TPU v7x, 32 devices: a whole 2x2x4 slice. The times are simulated.
32 devices in a mesh: dp: 8 (over z, core), expert: 4 (over y, x).
Axes of the slice: x: 2, y: 2, z: 4, core: 2. Of those that a mesh axis runs over, the one named last changes fastest.
Arguments:
- tokens: bfloat16 [4096, 2048], P(('dp', 'expert')), may hold values from -6 to 6
- upstream: bfloat16 [4096, 2048], P(('dp', 'expert')), may hold values from -6 to 6
- expert_ids: int32 [4096, 8], P(('dp', 'expert')), may hold values from 0 to 31, all different within a row; in each aligned block of 128 rows (0 to 127, 128 to 255, ...) at most 40 rows name the same one
- gate_weights: bfloat16 [4096, 8], P(('dp', 'expert')), may hold values from 0.049804688 to 0.5
- w_up: bfloat16 [4, 2048, 768], P('expert'), may hold values from -0.125 to 0.125
- w_down: bfloat16 [4, 768, 2048], P('expert'), may hold values from -0.21875 to 0.21875
Outputs:
- token_grads: bfloat16 [4096, 2048], P(('dp', 'expert'))
- gate_grads: bfloat16 [4096, 8], P(('dp', 'expert'))
- router_grads: float32 [4, 2048], P('expert')
Inputs may be any that keep to these rules, and one draw needn't show every extreme that they name: `expert_ids`: each row names 8 different experts; among the 128 rows of one device no expert is named by more than 40 rows.
All inputs are finite; a program needn't handle non-finite values.
Results may differ from a plain program's by a relative error of at most 0.0063.
Values may be sent and summed in bfloat16 or wider, within the bound.
A program may use at most 64 MiB of HBM per device.

v0:
```python
import jax
import jax.numpy as jnp
from jax import lax
from jax.sharding import PartitionSpec as P

EXP_DEV = 8


def forward_part(rows_x, up_mat, down_mat):
    act = jnp.dot(rows_x, up_mat, preferred_element_type=jnp.float32)
    sig = jax.nn.sigmoid(act)
    hidden = (act * sig).astype(jnp.bfloat16)
    expert_out = jnp.dot(hidden, down_mat, preferred_element_type=jnp.float32)
    return (act, sig, expert_out)


def scale_part(expert_out, rows_dy, rows_gate):
    dy_wide = rows_dy.astype(jnp.float32)
    gate_term = jnp.sum(dy_wide * expert_out, axis=1)
    scaled = (rows_gate.astype(jnp.float32)[:, None] * dy_wide).astype(jnp.bfloat16)
    return (gate_term, scaled)


def input_part(act, sig, scaled, up_mat, down_mat):
    back = lax.dot_general(
        scaled, down_mat, (((1,), (1,)), ((), ())), preferred_element_type=jnp.float32
    )
    act_grad = (back * sig * (1.0 + act * (1.0 - sig))).astype(jnp.bfloat16)
    return lax.dot_general(
        act_grad, up_mat, (((1,), (1,)), ((), ())), preferred_element_type=jnp.float32
    ).astype(jnp.bfloat16)


def router_total(local_col, column_tok):
    return lax.psum(local_col, "dp") / jnp.float32(column_tok)


def body(tokens, upstream, expert_ids, gate_weights, w_up, w_down):
    owners_count = lax.axis_size("expert")
    experts = EXP_DEV * owners_count
    tok_count = tokens.shape[0]
    top = expert_ids.shape[1]
    width = tokens.shape[1]
    column_tok = tok_count * lax.axis_size("dp")
    most = tok_count * top // experts + tok_count * top // (4 * experts)
    slots_all = owners_count * most
    up_mat = w_up[0]
    down_mat = w_down[0]
    flat_ids = expert_ids.reshape(-1)
    live = flat_ids % EXP_DEV == 0
    target = flat_ids // EXP_DEV
    onehot = ((target[:, None] == jnp.arange(owners_count)[None, :]) & live[:, None]).astype(
        jnp.int32
    )
    before = jnp.cumsum(onehot, axis=0) - onehot
    slot = jnp.sum(before * onehot, axis=1)
    place = jnp.where(live, target * most + slot, -1)
    route_pick = place[None, :] == jnp.arange(slots_all)[:, None]
    token_pick = jnp.any(route_pick.reshape(slots_all, tok_count, top), axis=2).astype(jnp.bfloat16)
    route_table = route_pick.astype(jnp.bfloat16)
    send_x = (
        jnp.dot(token_pick, tokens, preferred_element_type=jnp.float32)
        .astype(jnp.bfloat16)
        .reshape(owners_count, most, width)
    )
    send_dy = (
        jnp.dot(token_pick, upstream, preferred_element_type=jnp.float32)
        .astype(jnp.bfloat16)
        .reshape(owners_count, most, width)
    )
    send_gate = (
        jnp.dot(route_table, gate_weights.reshape(-1), preferred_element_type=jnp.float32)
        .astype(jnp.bfloat16)
        .reshape(owners_count, most)
    )
    rows_x = lax.all_to_all(send_x, "expert", split_axis=0, concat_axis=0, tiled=True)
    rows_dy = lax.all_to_all(send_dy, "expert", split_axis=0, concat_axis=0, tiled=True)
    rows_gate = lax.all_to_all(send_gate, "expert", split_axis=0, concat_axis=0, tiled=True)
    groups = rows_gate.shape[0]
    count = rows_gate.shape[1]
    flat_x = rows_x.reshape(groups * count, width)
    act, sig, expert_out = forward_part(flat_x, up_mat, down_mat)
    gate_term, scaled = scale_part(
        expert_out, rows_dy.reshape(groups * count, width), rows_gate.reshape(-1)
    )
    route_grad = input_part(act, sig, scaled, up_mat, down_mat)
    weighted = (gate_term[:, None] * flat_x.astype(jnp.float32)).reshape(groups, count, width)
    back_rows = lax.all_to_all(
        route_grad.reshape(groups, count, width), "expert", split_axis=0, concat_axis=0, tiled=True
    )
    back_gate = lax.all_to_all(
        gate_term.astype(jnp.bfloat16).reshape(groups, count),
        "expert",
        split_axis=0,
        concat_axis=0,
        tiled=True,
    )
    back_rows, back_gate, weighted_all = (back_rows, back_gate, weighted)
    router_grads = router_total(jnp.sum(weighted_all, axis=(0, 1)), column_tok)
    token_grads = lax.dot_general(
        token_pick,
        back_rows.reshape(slots_all, width),
        (((0,), (0,)), ((), ())),
        preferred_element_type=jnp.float32,
    ).astype(jnp.bfloat16)
    gate_flat = lax.dot_general(
        route_table,
        back_gate.reshape(slots_all),
        (((0,), (0,)), ((), ())),
        preferred_element_type=jnp.float32,
    )
    gate_grads = gate_flat.reshape(tok_count, top).astype(jnp.bfloat16)
    return (token_grads, gate_grads, router_grads[None])


def solution(mesh):
    return jax.shard_map(
        body,
        mesh=mesh,
        in_specs=(
            P(("dp", "expert"), None),
            P(("dp", "expert"), None),
            P(("dp", "expert"), None),
            P(("dp", "expert"), None),
            P("expert", None, None),
            P("expert", None, None),
        ),
        out_specs=(P(("dp", "expert"), None), P(("dp", "expert"), None), P("expert", None)),
        check_vma=False,
    )
```

profile of v0, /device:TPU:0, one launch (start us, length us, event | category | flops | bytes accessed | tf_op | source)
XLA Modules:
  0.0 77.3 jit_solution(12351207888736167650)
XLA Ops:
  0.6 0.9 %copy.38 = s32[128,8]{1,0:T(8,128)S(1)} copy(s32[128,8]{0,1:T(8,128)} %param.8) | data formatting | bytes 8192 | tf_op args[2]
  1.8 0.8 %copy.45 = bf16[128,8]{1,0:T(8,128)(2,1)S(1)} copy(bf16[128,8]{0,1:T(8,128)(2,1)} %param.9) | data formatting | bytes 4096 | tf_op args[3]
  2.7 1.1 %reduce-window.6 = s32[4,8,128]{2,1,0:T(8,128)S(1)} reduce-window(s32[4,8,128]{2,1,0:T(8,128)S(1)} %fusion.52, s32[]{:T(128)} %constant.37.clone.1), window={size=1x1x128 pad=0_0x0_0x127_0}, to_apply=%region_0.1 | reduce-window | flops 520192 | bytes 32772 | tf_op jit(solution)/shard_map/reduce-window
  4.7 0.7 all_to_all.25
  5.3 5.2 %all-to-all-start = ((bf16[4,1,40]{2,1,0:T(2,128)(2,1)}), bf16[4,1,40]{2,1,0:T(2,128)(2,1)S(1)}, u32[]{:S(2)}, u32[]{:S(2)}) async-start(bf16[4,1,40]{2,1,0:T(2,128)(2,1)} %all_to_all.25), calls=%async_computation | async-start | bytes 4096 | tf_op jit(solution)/shard_map/all_to_all | solution.py:78
  11.0 2.2 %convolution_convert_fusion = bf16[160,2048]{1,0:T(8,128)(2,1)} fusion(pred[160,128]{1,0:T(8,128)(4,1)S(1)} %fusion.28, bf16[128,2048]{1,0:T(8,128)(2,1)} %param.6), kind=kOutput, calls=%fused_computation.10 | convolution fusion | flops 84213760 | bytes 1200128 | tf_op jit(solution)/shard_map/dot_general | solution.py:62
  13.2 1.9 %all-to-all-done = bf16[4,1,40]{2,1,0:T(2,128)(2,1)S(1)} async-done(((bf16[4,1,40]{2,1,0:T(2,128)(2,1)}), bf16[4,1,40]{2,1,0:T(2,128)(2,1)S(1)}, u32[]{:S(2)}, u32[]{:S(2)}) %all-to-all-start) | async-done | bytes 352 | tf_op jit(solution)/shard_map/all_to_all | solution.py:78
  15.1 4.2 %all-to-all-start.2 = ((bf16[4,40,2048]{2,1,0:T(8,128)(2,1)}), bf16[4,40,2048]{2,1,0:T(8,128)(2,1)}, u32[]{:S(2)}, u32[]{:S(2)}) async-start(bf16[4,40,2048]{2,1,0:T(8,128)(2,1)} %bitcast.73), calls=%async_computation.2 | async-start | bytes 1310720 | tf_op jit(solution)/shard_map/all_to_all | solution.py:76
  19.2 2.2 %convolution_convert_fusion.1 = bf16[160,2048]{1,0:T(8,128)(2,1)} fusion(pred[160,128]{1,0:T(8,128)(4,1)S(1)} %fusion.28, bf16[128,2048]{1,0:T(8,128)(2,1)} %param.7), kind=kOutput, calls=%fused_computation.11 | convolution fusion | flops 84213760 | bytes 1200128 | tf_op jit(solution)/shard_map/dot_general | solution.py:67
  21.4 6.1 %all-to-all-done.2 = bf16[4,40,2048]{2,1,0:T(8,128)(2,1)} async-done(((bf16[4,40,2048]{2,1,0:T(8,128)(2,1)}), bf16[4,40,2048]{2,1,0:T(8,128)(2,1)}, u32[]{:S(2)}, u32[]{:S(2)}) %all-to-all-start.2) | async-done | bytes 655392 | tf_op jit(solution)/shard_map/all_to_all | solution.py:76
  27.6 4.2 %all-to-all-start.1 = ((bf16[4,40,2048]{2,1,0:T(8,128)(2,1)}), bf16[4,40,2048]{2,1,0:T(8,128)(2,1)}, u32[]{:S(2)}, u32[]{:S(2)}) async-start(bf16[4,40,2048]{2,1,0:T(8,128)(2,1)} %bitcast.72), calls=%async_computation.1 | async-start | bytes 1310720 | tf_op jit(solution)/shard_map/all_to_all | solution.py:77
  31.7 2.5 %fusion.2 = f32[160,768]{1,0:T(8,128)} fusion(bf16[160,2048]{1,0:T(8,128)(2,1)} %bitcast.7, bf16[1,2048,768]{2,1,0:T(8,128)(2,1)S(1)} %copy-done), kind=kOutput, calls=%fused_computation.2 | convolution fusion | flops 503316480 | bytes 4292608 | tf_op jit(solution)/shard_map/dot_general | solution.py:10
  34.3 5.3 %all-to-all-done.1 = bf16[4,40,2048]{2,1,0:T(8,128)(2,1)} async-done(((bf16[4,40,2048]{2,1,0:T(8,128)(2,1)}), bf16[4,40,2048]{2,1,0:T(8,128)(2,1)}, u32[]{:S(2)}, u32[]{:S(2)}) %all-to-all-start.1) | async-done | bytes 655392 | tf_op jit(solution)/shard_map/all_to_all | solution.py:77
  39.6 3.0 %fusion.14 = f32[160]{0:T(256)S(1)} fusion(bf16[1,768,2048]{2,1,0:T(8,128)(2,1)} %param.11, f32[160,768]{1,0:T(8,128)} %fusion.2, bf16[160,2048]{1,0:T(8,128)(2,1)} %bitcast.60), kind=kOutput, calls=%fused_computation.15 | convolution fusion | flops 504913760 | bytes 4293248 | tf_op jit(solution)/shard_map/dot_general | solution.py:13
  42.6 0.7 convert_element_type.98
  43.3 3.2 %all-to-all-start.4 = ((bf16[4,1,40]{2,1,0:T(2,128)(2,1)}), bf16[4,1,40]{2,1,0:T(2,128)(2,1)S(1)}, u32[]{:S(2)}, u32[]{:S(2)}) async-start(bf16[4,1,40]{2,1,0:T(2,128)(2,1)} %convert_element_type.98), calls=%async_computation.4 | async-start | bytes 4096 | tf_op jit(solution)/shard_map/all_to_all | solution.py:91
  46.5 2.1 %multiply_convert_fusion = bf16[4,40,2048]{2,1,0:T(8,128)(2,1)} fusion(f32[4,40]{1,0:T(4,128)S(1)} %bitcast.76, bf16[4,40,2048]{2,1,0:T(8,128)(2,1)} %all-to-all-done.1), kind=kLoop, calls=%fused_computation.14 | loop fusion | flops 983040 | bytes 1311360 | tf_op jit(solution)/shard_map/convert_element_type | solution.py:20
  48.6 5.4 %fusion.11 = bf16[160,2048]{1,0:T(8,128)(2,1)} fusion(bf16[1,2048,768]{2,1,0:T(8,128)(2,1)S(1)} %copy-done, bf16[160,2048]{1,0:T(8,128)(2,1)} %bitcast.75, bf16[1,768,2048]{2,1,0:T(8,128)(2,1)} %param.11, f32[160,768]{1,0:T(8,128)} %fusion.2), kind=kOutput, calls=%fused_computation.9 | convolution fusion | flops 1008066560 | bytes 8093696 | tf_op jit(solution)/shard_map/dot_general | solution.py:29
  54.1 4.2 %all-to-all-start.3 = ((bf16[4,40,2048]{2,1,0:T(8,128)(2,1)}), bf16[4,40,2048]{2,1,0:T(8,128)(2,1)}, u32[]{:S(2)}, u32[]{:S(2)}) async-start(bf16[4,40,2048]{2,1,0:T(8,128)(2,1)} %bitcast.74), calls=%async_computation.3 | async-start | bytes 1310720 | tf_op jit(solution)/shard_map/all_to_all | solution.py:88
  58.3 1.3 %multiply_reduce_fusion = f32[2048]{0:T(1024)S(1)} fusion(bf16[4,40,2048]{2,1,0:T(8,128)(2,1)} %all-to-all-done.2, f32[4,40]{1,0:T(4,128)S(1)} %mul.66), kind=kLoop, calls=%fused_computation.13 | loop fusion | flops 980992 | bytes 664192 | tf_op jit(solution)/shard_map/reduce_sum | solution.py:99
  59.6 14.0 %psum.7 = f32[2048]{0:T(1024)S(1)} all-reduce(f32[2048]{0:T(1024)S(1)} %multiply_reduce_fusion), channel_id=1, replica_groups=mesh['dp'=8,'expert'=4] {'dp'}, use_global_device_ids=true, to_apply=%region_6.7 | all-reduce | flops 2048 | bytes 16384 | tf_op jit(solution)/shard_map/psum | solution.py:35
  73.6 0.6 broadcast_multiply_fusion
  74.5 0.6 convert_element_type.94
  75.1 2.2 %convolution_convert_fusion.2 = bf16[128,2048]{1,0:T(8,128)(2,1)} fusion(pred[160,128]{1,0:T(8,128)(4,1)S(1)} %fusion.28, bf16[160,2048]{1,0:T(8,128)(2,1)} %bitcast.10), kind=kOutput, calls=%fused_computation.12 | convolution fusion | flops 84148224 | bytes 1200128 | tf_op jit(solution)/shard_map/dot_general | solution.py:100
  (29 shorter events, 1.9 us)
Async XLA Ops:
  0.6 31.1 %copy-start = (bf16[1,2048,768]{2,1,0:T(8,128)(2,1)S(1)}, bf16[1,2048,768]{2,1,0:T(8,128)(2,1)}, u32[]{:S(2)}) copy-start(bf16[1,2048,768]{2,1,0:T(8,128)(2,1)} %param.10) | copy-start | bytes 9437188
  5.3 9.7 %all-to-all-start = ((bf16[4,1,40]{2,1,0:T(2,128)(2,1)}), bf16[4,1,40]{2,1,0:T(2,128)(2,1)S(1)}, u32[]{:S(2)}, u32[]{:S(2)}) async-start(bf16[4,1,40]{2,1,0:T(2,128)(2,1)} %all_to_all.25), calls=%async_computation | async-start | bytes 4096 | tf_op jit(solution)/shard_map/all_to_all | solution.py:78
  15.1 12.5 %all-to-all-start.2 = ((bf16[4,40,2048]{2,1,0:T(8,128)(2,1)}), bf16[4,40,2048]{2,1,0:T(8,128)(2,1)}, u32[]{:S(2)}, u32[]{:S(2)}) async-start(bf16[4,40,2048]{2,1,0:T(8,128)(2,1)} %bitcast.73), calls=%async_computation.2 | async-start | bytes 1310720 | tf_op jit(solution)/shard_map/all_to_all | solution.py:76
  27.6 12.0 %all-to-all-start.1 = ((bf16[4,40,2048]{2,1,0:T(8,128)(2,1)}), bf16[4,40,2048]{2,1,0:T(8,128)(2,1)}, u32[]{:S(2)}, u32[]{:S(2)}) async-start(bf16[4,40,2048]{2,1,0:T(8,128)(2,1)} %bitcast.72), calls=%async_computation.1 | async-start | bytes 1310720 | tf_op jit(solution)/shard_map/all_to_all | solution.py:77
  43.3 10.9 %all-to-all-start.4 = ((bf16[4,1,40]{2,1,0:T(2,128)(2,1)}), bf16[4,1,40]{2,1,0:T(2,128)(2,1)S(1)}, u32[]{:S(2)}, u32[]{:S(2)}) async-start(bf16[4,1,40]{2,1,0:T(2,128)(2,1)} %convert_element_type.98), calls=%async_computation.4 | async-start | bytes 4096 | tf_op jit(solution)/shard_map/all_to_all | solution.py:91
  54.1 21.0 %all-to-all-start.3 = ((bf16[4,40,2048]{2,1,0:T(8,128)(2,1)}), bf16[4,40,2048]{2,1,0:T(8,128)(2,1)}, u32[]{:S(2)}, u32[]{:S(2)}) async-start(bf16[4,40,2048]{2,1,0:T(8,128)(2,1)} %bitcast.74), calls=%async_computation.3 | async-start | bytes 1310720 | tf_op jit(solution)/shard_map/all_to_all | solution.py:88
where the time goes:
time: 78 us; the launch traced here: 77.3 us
  starting transfers between devices  20.9 us (27%)
  matrix products  18 us (23%)
  blocking collectives  14 us (18%)
  waiting for transfers between devices  13.3 us (17%)
  other arithmetic  6.46 us (8%)
  local copies, waits for them, and re-layouts  3.89 us (5%)
  between operations  0.78 us (1%)
    psum x1, blocking collectives, router_total(): return lax.psum(local_col, 'dp') / jnp.float32(column_tok)  14 us
    all_to_all x1, waiting for transfers between devices, body(): lax.all_to_all(send_x, 'expert', split_axis=0, concat_axis=0, tiled=True)  6.1 us
    dot_general x1, matrix products, input_part(): lax.dot_general(act_grad, up_mat, (((1,), (1,)), ((), ())), preferred_ele...  5.42 us
    all_to_all x1, waiting for transfers between devices, body(): lax.all_to_all(send_dy, 'expert', split_axis=0, concat_axis=0, tiled=True)  5.31 us
    all_to_all x1, starting transfers between devices, body(): lax.all_to_all(send_gate, 'expert', split_axis=0, concat_axis=0, tiled=True)  5.16 us
    all_to_all x1, starting transfers between devices, body(): lax.all_to_all(route_grad.reshape(groups, count, width), 'expert', split_...  4.17 us
    all_to_all x1, starting transfers between devices, body(): lax.all_to_all(send_dy, 'expert', split_axis=0, concat_axis=0, tiled=True)  4.16 us
    all_to_all x1, starting transfers between devices, body(): lax.all_to_all(send_x, 'expert', split_axis=0, concat_axis=0, tiled=True)  4.15 us
  transfers between devices with their start and end apart: 5, of which 3 were waited for; matrix products, arithmetic and copies ran while one was open for 23% of the time, Pallas kernels for 0%

commit v1 on v0

v1 whole, which is shorter than its diff:
```python
import functools
import jax
import jax.numpy as jnp
from jax import lax
from jax.experimental import pallas as pl
from jax.experimental.pallas import tpu as pltpu
from jax.sharding import PartitionSpec as P

EXP_DEV = 8
MESH = pl.DeviceIdType.MESH
F32 = jnp.float32
BF16 = jnp.bfloat16


def nt_dot(a, b):
    return lax.dot_general(a, b, (((1,), (1,)), ((), ())), preferred_element_type=F32)


def flipped(me, j):
    out, bit = me, 1
    while bit <= j:
        if (j // bit) % 2:
            out = out + bit - 2 * bit * ((me // bit) % 2)
        bit *= 2
    return out


def kernel(n, dp, rows, groups, tok_hbm, dy_hbm, ids_ref, gate_ref, wu_hbm, wd_hbm,
           tg_ref, gg_ref, rg_ref,
           tok, dy, wu, wd, send, recv, rsend, rrecv, gsend, grecv, agr, cols, gl, gr,
           local_sem, s_send, s_recv, r_send, r_recv, g_send, g_recv, c_send, c_recv):
    me = lax.axis_index("expert")
    my_dp = lax.axis_index("dp")
    tok_count, width = tok.shape
    hidden = wu.shape[1]
    top = ids_ref.shape[1]
    half = width // 2
    hi = -(-rows // 16) * 16
    lo = rows // 16 * 16
    off = rows - lo
    span = 2 * rows - lo
    peers = [flipped(me, j) for j in range(n)]

    loads = [
        pltpu.make_async_copy(src, dst, local_sem.at[i])
        for i, (src, dst) in enumerate(
            ((tok_hbm, tok), (dy_hbm, dy), (wu_hbm, wu), (wd_hbm, wd)))
    ]
    for load in loads:
        load.start()

    barrier = pltpu.get_barrier_semaphore()
    for j in range(1, n):
        pl.semaphore_signal(barrier, inc=1, device_id=(my_dp, peers[j]), device_id_type=MESH)
    for k in range(1, dp):
        pl.semaphore_signal(
            barrier, inc=1, device_id=(lax.rem(my_dp + k, dp), me), device_id_type=MESH)

    ids = ids_ref[...]
    gates = gate_ref[...].astype(F32)
    lane = lax.broadcasted_iota(jnp.int32, (1, 128), 1)
    target = jnp.full((1, 128), -1, jnp.int32)
    for j in range(n):
        target = jnp.where(lane == j, EXP_DEV * peers[j], target)
    hit = jnp.zeros((tok_count, 128), F32)
    gsel = jnp.zeros((tok_count, 128), F32)
    for k in range(top):
        same = ids[:, k:k + 1] == target
        hit = hit + jnp.where(same, 1.0, 0.0)
        gsel = gsel + jnp.where(same, gates[:, k:k + 1], 0.0)
    t_row = lax.broadcasted_iota(jnp.int32, (tok_count, tok_count), 0)
    t_col = lax.broadcasted_iota(jnp.int32, (tok_count, tok_count), 1)
    below = jnp.where(t_col < t_row, 1.0, 0.0).astype(BF16)
    eye = jnp.where(t_col == t_row, 1.0, 0.0).astype(BF16)
    rank = jnp.dot(below, hit.astype(BF16), preferred_element_type=F32)
    key = jnp.where(hit > 0.5, rank, -1.0)
    key_t = lax.dot_general(
        key.astype(BF16), eye, (((0,), (0,)), ((), ())), preferred_element_type=F32)

    row_id = lax.broadcasted_iota(jnp.int32, (rows, tok_count), 0).astype(F32)
    picks = [
        jnp.where(row_id == key_t[j:j + 1, :], 1.0, 0.0)
        for j in range(n)
    ]
    pick_all = jnp.concatenate(picks, axis=0).astype(BF16)
    loads[0].wait()
    loads[1].wait()
    for c in range(0, width, 512):
        sel_x = jnp.dot(pick_all, tok[:, c:c + 512], preferred_element_type=F32)
        sel_d = jnp.dot(pick_all, dy[:, c:c + 512], preferred_element_type=F32)
        for j in range(n):
            both = jnp.concatenate(
                [sel_x[j * rows:(j + 1) * rows], sel_d[j * rows:(j + 1) * rows]], axis=0)
            if j == 0:
                recv[0, :, c:c + 512] = both.astype(BF16)
            else:
                send[j, :, c:c + 512] = both.astype(BF16)

    pl.semaphore_wait(barrier, n - 1 + dp - 1)

    def remote(src, dst, a_sem, b_sem, j):
        return pltpu.make_async_remote_copy(
            src_ref=src.at[j], dst_ref=dst.at[j], send_sem=a_sem.at[j], recv_sem=b_sem.at[j],
            device_id=(my_dp, peers[j]), device_id_type=MESH)

    out_copies = [None] + [remote(send, recv, s_send, s_recv, j) for j in range(1, n)]
    for j in range(1, n):
        out_copies[j].start()

    lanes = lax.broadcasted_iota(jnp.int32, (1, n * hi), 1).astype(F32)
    mat = jnp.zeros((tok_count, n * hi), F32)
    mat_r = jnp.zeros((tok_count, n * span), F32)
    lanes_r = lax.broadcasted_iota(jnp.int32, (1, n * span), 1).astype(F32)
    for j in range(n):
        there = hit[:, j:j + 1] > 0.5
        spot = jnp.where(there, rank[:, j:j + 1] + (hi * j), -1.0)
        mat = mat + jnp.where(lanes == spot, gsel[:, j:j + 1], 0.0)
        spot_r = jnp.where(there, rank[:, j:j + 1] + (span * j + off), -1.0)
        mat_r = mat_r + jnp.where(lanes_r == spot_r, gsel[:, j:j + 1], 0.0)
    gl[...] = mat.astype(BF16)
    gr[...] = mat_r.astype(BF16)

    loads[2].wait()
    loads[3].wait()
    diag = (lax.broadcasted_iota(jnp.int32, (rows, 128), 0)
            == lax.broadcasted_iota(jnp.int32, (rows, 128), 1))
    total = jnp.zeros((1, width), F32)
    back_copies = []
    for group in groups:
        for j in group:
            if j:
                out_copies[j].wait_recv()
        g = len(group)
        xs = jnp.concatenate([recv[j, 0:hi, :] for j in group], axis=0)
        ds = jnp.concatenate([recv[j, lo:2 * rows, :] for j in group], axis=0)
        terms = [jnp.zeros((rows, 1), F32) for _ in group]
        for c in range(0, hidden, 256):
            act_all = jnp.dot(xs, wu[:, c:c + 256], preferred_element_type=F32)
            u_all = nt_dot(ds, wd[c:c + 256, :])
            grads = []
            for i in range(g):
                act = act_all[i * hi:i * hi + rows]
                u = u_all[i * span + off:i * span + off + rows]
                sig = jax.nn.sigmoid(act)
                hid = (act * sig).astype(BF16).astype(F32)
                terms[i] = terms[i] + jnp.sum(hid * u, axis=1, keepdims=True)
                grads.append(u * sig * (1.0 + act * (1.0 - sig)))
            agr[0:g * rows, c:c + 256] = jnp.concatenate(grads, axis=0).astype(BF16)
        grad_in = agr[0:g * rows, :]
        left = nt_dot(grad_in, wu[0:half, :])
        right = nt_dot(grad_in, wu[half:width, :])
        for i, j in enumerate(group):
            block = jnp.concatenate(
                [left[i * rows:(i + 1) * rows], right[i * rows:(i + 1) * rows]], axis=0)
            line = jnp.sum(jnp.where(diag, terms[i], 0.0), axis=0, keepdims=True)
            line = jnp.broadcast_to(line, (8, 128))
            if j == 0:
                rrecv[0] = block.astype(BF16)
                grecv[0] = line
            else:
                rsend[j] = block.astype(BF16)
                gsend[j] = line
                for args in ((rsend, rrecv, r_send, r_recv), (gsend, grecv, g_send, g_recv)):
                    copy = remote(*args, j)
                    copy.start()
                    back_copies.append(copy)
        for i, j in enumerate(group):
            total = total + jnp.sum(
                recv[j, 0:hi, :].astype(F32)[0:rows] * terms[i], axis=0, keepdims=True)

    cols[my_dp] = total
    col_copies = []
    for k in range(1, dp):
        copy = pltpu.make_async_remote_copy(
            src_ref=cols.at[my_dp], dst_ref=cols.at[my_dp], send_sem=c_send.at[k],
            recv_sem=c_recv.at[k], device_id=(lax.rem(my_dp + k, dp), me), device_id_type=MESH)
        copy.start()
        col_copies.append(copy)

    for k in range(1, dp):
        src = lax.rem(my_dp + dp - k, dp)
        pltpu.make_async_remote_copy(
            src_ref=cols.at[src], dst_ref=cols.at[src], send_sem=c_send.at[k],
            recv_sem=c_recv.at[k], device_id=(src, me), device_id_type=MESH).wait_recv()
    col = cols[0]
    for i in range(1, dp):
        col = col + cols[i]
    rg_ref[...] = col / F32(tok_count * dp)

    for copy in back_copies:
        copy.wait_recv()
    back_l = jnp.concatenate([rrecv[j, 0:hi, :] for j in range(n)], axis=0)
    tg_ref[:, 0:half] = jnp.dot(gl[...], back_l, preferred_element_type=F32).astype(BF16)
    back_r = jnp.concatenate([rrecv[j, lo:2 * rows, :] for j in range(n)], axis=0)
    tg_ref[:, half:width] = jnp.dot(gr[...], back_r, preferred_element_type=F32).astype(BF16)

    gate_out = jnp.zeros((tok_count, top), F32)
    lane_f = lane.astype(F32)
    for j in range(n):
        term = jnp.sum(
            jnp.where(lane_f == key[:, j:j + 1], grecv[j, 0:1, :], 0.0), axis=1, keepdims=True)
        gate_out = gate_out + jnp.where(ids == EXP_DEV * peers[j], term, 0.0)
    gg_ref[...] = gate_out.astype(BF16)

    for copy in out_copies[1:] + back_copies + col_copies:
        copy.wait_send()


def body(tokens, upstream, expert_ids, gate_weights, w_up, w_down):
    n = lax.axis_size("expert")
    dp = lax.axis_size("dp")
    tok_count, width = tokens.shape
    top = expert_ids.shape[1]
    hidden = w_up.shape[2]
    experts = EXP_DEV * n
    most = tok_count * top // experts + tok_count * top // (4 * experts)
    rows = -(-most // 8) * 8
    hi = -(-rows // 16) * 16
    span = 2 * rows - rows // 16 * 16
    groups = [(0,), tuple(range(1, n // 2 + 1)), tuple(range(n // 2 + 1, n))]
    biggest = max(len(g) for g in groups)
    hbm = pl.BlockSpec(memory_space=pl.ANY)
    vmem = pl.BlockSpec(memory_space=pltpu.VMEM)
    dma = pltpu.SemaphoreType.DMA
    return pl.pallas_call(
        functools.partial(kernel, n, dp, rows, groups),
        out_shape=(
            jax.ShapeDtypeStruct((tok_count, width), BF16),
            jax.ShapeDtypeStruct((tok_count, top), BF16),
            jax.ShapeDtypeStruct((1, width), F32),
        ),
        in_specs=[hbm, hbm, vmem, vmem, hbm, hbm],
        out_specs=(vmem, vmem, vmem),
        scratch_shapes=[
            pltpu.VMEM((tok_count, width), BF16),
            pltpu.VMEM((tok_count, width), BF16),
            pltpu.VMEM((width, hidden), BF16),
            pltpu.VMEM((hidden, width), BF16),
            pltpu.VMEM((n, 2 * rows, width), BF16),
            pltpu.VMEM((n, 2 * rows, width), BF16),
            pltpu.VMEM((n, 2 * rows, width // 2), BF16),
            pltpu.VMEM((n, 2 * rows, width // 2), BF16),
            pltpu.VMEM((n, 8, 128), F32),
            pltpu.VMEM((n, 8, 128), F32),
            pltpu.VMEM((-(-biggest * rows // 16) * 16, hidden), BF16),
            pltpu.VMEM((dp, 1, width), F32),
            pltpu.VMEM((tok_count, n * hi), BF16),
            pltpu.VMEM((tok_count, n * span), BF16),
            dma((4,)),
            dma((n,)), dma((n,)), dma((n,)), dma((n,)), dma((n,)), dma((n,)),
            dma((dp,)), dma((dp,)),
        ],
        compiler_params=pltpu.CompilerParams(
            collective_id=0, has_side_effects=True, vmem_limit_bytes=48 * 1024 * 1024),
        cost_estimate=pl.CostEstimate(
            flops=6 * n * rows * width * hidden, bytes_accessed=4 * width * hidden,
            transcendentals=n * rows * hidden),
    )(tokens, upstream, expert_ids, gate_weights, w_up[0], w_down[0])


def solution(mesh):
    return jax.shard_map(
        body,
        mesh=mesh,
        in_specs=(
            P(("dp", "expert"), None),
            P(("dp", "expert"), None),
            P(("dp", "expert"), None),
            P(("dp", "expert"), None),
            P("expert", None, None),
            P("expert", None, None),
        ),
        out_specs=(P(("dp", "expert"), None), P(("dp", "expert"), None), P("expert", None)),
        check_vma=False,
    )
```

time: 78 us -> 39.7 us (0.51)
  Pallas kernels: 0 us -> 31.1 us
  starting transfers between devices: 20.9 us -> 0 us
  matrix products: 18 us -> 0 us
  blocking collectives: 14 us -> 0 us
  waiting for transfers between devices: 13.3 us -> 0 us
  other arithmetic: 6.46 us -> 0 us
  local copies, waits for them, and re-layouts: 3.89 us -> 7.6 us
    pallas_call x0 -> x1, Pallas kernels: none -> 31.1 us  [body(): pl.pallas_call(functools.partial(kernel, n, dp, rows, groups), out_shape=...]
    all_to_all x5 -> x0, starting transfers between devices: 20.9 us -> none  [the longest x1 5.16 us: body(): lax.all_to_all(send_gate, 'expert', split_axis=0, concat_axis=0, tiled=True)]
    dot_general x8 -> x0, matrix products: 18 us -> none  [the longest x1 5.42 us: input_part(): lax.dot_general(act_grad, up_mat, (((1,), (1,)), ((), ())), preferred_ele...]
    psum x1 -> x0, blocking collectives: 14 us -> none  [router_total(): return lax.psum(local_col, 'dp') / jnp.float32(column_tok)]
    all_to_all x5 -> x0, waiting for transfers between devices: 13.3 us -> none  [the longest x1 6.1 us: body(): lax.all_to_all(send_x, 'expert', split_axis=0, concat_axis=0, tiled=True)]
    unnamed x4 -> x10, local copies, waits for them, and re-layouts: 1.75 us -> 6.95 us
    convert_element_type x6 -> x0, other arithmetic: 2.73 us -> none  [the longest x1 2.13 us: scale_part(): (rows_gate.astype(jnp.float32)[:, None] * dy_wide).astype(jnp.bfloat16)]
    another operation x2 -> x0, other arithmetic: 1.33 us -> none
  transfers between devices with their start and end apart: 5 -> 0, of which waited for: 3 -> 0; matrix products, arithmetic and copies ran while one was open for 23% -> 0% of each run, Pallas kernels for 0% -> 0%
where the time goes in v1:
time: 39.7 us; the launch traced here: 39.4 us
  Pallas kernels  31.1 us (78%)
  local copies, waits for them, and re-layouts  7.6 us (19%)
  between operations  0.65 us (2%)
    pallas_call x1, Pallas kernels, body(): pl.pallas_call(functools.partial(kernel, n, dp, rows, groups), out_shape=...  31.1 us
    unnamed x10, local copies, waits for them, and re-layouts  6.95 us

profile of v1, /device:TPU:0, one launch (start us, length us, event | category | flops | bytes accessed | tf_op | source)
XLA Modules:
  0.0 39.4 jit_solution(14521096992427622996)
XLA Ops:
  0.6 0.8 %copy.10.gate_ref = bf16[128,8]{1,0:T(8,128)(2,1)S(1)} copy(bf16[128,8]{0,1:T(8,128)(2,1)} %param.9) | data formatting | bytes 4096 | tf_op args[3]
  1.4 0.8 %copy.9.ids_ref = s32[128,8]{1,0:T(8,128)S(1)} copy(s32[128,8]{0,1:T(8,128)} %param.8) | data formatting | bytes 8192 | tf_op args[2]
  2.2 0.0 copy-start
  2.2 1.9 %copy-done = bf16[1,2048,768]{2,1,0:T(8,128)(2,1)S(1)} copy-done((bf16[1,2048,768]{2,1,0:T(8,128)(2,1)S(1)}, bf16[1,2048,768]{2,1,0:T(8,128)(2,1)}, u32[]{:S(2)}) %copy-start) | copy-done | bytes 3145752
  4.1 0.0 copy-start.1
  4.1 1.0 %copy-done.1 = bf16[128,2048]{1,0:T(8,128)(2,1)S(1)} copy-done((bf16[128,2048]{1,0:T(8,128)(2,1)S(1)}, bf16[128,2048]{1,0:T(8,128)(2,1)}, u32[]{:S(2)}) %copy-start.1) | copy-done | bytes 524312
  5.2 0.0 copy-start.2
  5.2 1.0 %copy-done.2 = bf16[128,2048]{1,0:T(8,128)(2,1)S(1)} copy-done((bf16[128,2048]{1,0:T(8,128)(2,1)S(1)}, bf16[128,2048]{1,0:T(8,128)(2,1)}, u32[]{:S(2)}) %copy-start.2) | copy-done | bytes 524312
  6.2 31.1 %shard_map.85 = (bf16[128,2048]{1,0:T(8,128)(2,1)S(1)}, bf16[128,8]{1,0:T(8,128)(2,1)S(1)}, f32[1,2048]{1,0:T(1,128)S(1)}) custom-call(bf16[128,2048]{1,0:T(8,128)(2,1)S(1)} %copy-done.1, bf16[128,2048]{1,0:T(8,128)(2,1)S(1)} %copy-done.2, s32[128,8]{1,0:T(8,128)S(1)} %copy.9.ids_ref, bf16[128,8]{1,0:T(8,128)(2,1)S(1)} %copy.10.gate_ref, ...), custom_call_target="tpu_custom_call" | custom-call | flops 1509949440 | bytes 6291456 | tf_op jit(solution)/shard_map/pallas_call | solution.py:225
  37.3 0.7 %copy.11 = bf16[128,8]{0,1:T(8,128)(2,1)} copy(bf16[128,8]{1,0:T(8,128)(2,1)S(1)} %get-tuple-element.4) | data formatting | bytes 4096 | tf_op jit(solution)/shard_map/pallas_call | solution.py:225
  38.0 0.8 %copy.14 = bf16[128,2048]{1,0:T(8,128)(2,1)} copy(bf16[128,2048]{1,0:T(8,128)(2,1)S(1)} %get-tuple-element.9) | data formatting | bytes 1048576
  38.8 0.6 %copy.15 = f32[1,2048]{1,0:T(1,128)} copy(f32[1,2048]{1,0:T(1,128)S(1)} %get-tuple-element.11) | data formatting | bytes 16384
Async XLA Ops:
  2.2 1.9 %copy-start = (bf16[1,2048,768]{2,1,0:T(8,128)(2,1)S(1)}, bf16[1,2048,768]{2,1,0:T(8,128)(2,1)}, u32[]{:S(2)}) copy-start(bf16[1,2048,768]{2,1,0:T(8,128)(2,1)} %param.10) | copy-start | bytes 9437188
  4.1 1.0 %copy-start.1 = (bf16[128,2048]{1,0:T(8,128)(2,1)S(1)}, bf16[128,2048]{1,0:T(8,128)(2,1)}, u32[]{:S(2)}) copy-start(bf16[128,2048]{1,0:T(8,128)(2,1)} %tok_hbm.1) | copy-start | bytes 1572868
  5.2 1.0 %copy-start.2 = (bf16[128,2048]{1,0:T(8,128)(2,1)S(1)}, bf16[128,2048]{1,0:T(8,128)(2,1)}, u32[]{:S(2)}) copy-start(bf16[128,2048]{1,0:T(8,128)(2,1)} %dy_hbm.1) | copy-start | bytes 1572868

commit v2 on v1

v2 whole, which is shorter than its diff:
```python
import functools
import jax
import jax.numpy as jnp
from jax import lax
from jax.experimental import pallas as pl
from jax.experimental.pallas import tpu as pltpu
from jax.sharding import PartitionSpec as P

EXP_DEV = 8
MESH = pl.DeviceIdType.MESH
F32 = jnp.float32
BF16 = jnp.bfloat16


def nt_dot(a, b):
    return lax.dot_general(a, b, (((1,), (1,)), ((), ())), preferred_element_type=F32)


def flipped(me, j):
    out, bit = me, 1
    while bit <= j:
        if (j // bit) % 2:
            out = out + bit - 2 * bit * ((me // bit) % 2)
        bit *= 2
    return out


def kernel(n, dp, rows, groups, tok_hbm, dy_hbm, ids_ref, gate_ref, wu_hbm, wd_hbm,
           rrecv, gl, gr, gg_ref, rg_ref,
           tok, dy, wu, wd, send, recv, rsend, gsend, grecv, agr, cols, pick,
           local_sem, s_send, s_recv, r_send, r_recv, g_send, g_recv, c_send, c_recv):
    me = lax.axis_index("expert")
    my_dp = lax.axis_index("dp")
    tok_count, width = tok.shape
    hidden = wu.shape[1]
    half = width // 2
    hi = -(-rows // 16) * 16
    lo = rows // 16 * 16
    off = rows - lo
    span = 2 * rows - lo
    peers = [flipped(me, j) for j in range(n)]

    loads = [
        pltpu.make_async_copy(src, dst, local_sem.at[i])
        for i, (src, dst) in enumerate(
            ((tok_hbm, tok), (dy_hbm, dy), (wu_hbm, wu), (wd_hbm, wd)))
    ]
    for load in loads:
        load.start()

    barrier = pltpu.get_barrier_semaphore()
    for j in range(1, n):
        pl.semaphore_signal(barrier, inc=1, device_id=(my_dp, peers[j]), device_id_type=MESH)
    for k in range(1, dp):
        pl.semaphore_signal(
            barrier, inc=1, device_id=(lax.rem(my_dp + k, dp), me), device_id_type=MESH)

    ids = ids_ref[...]
    gates = gate_ref[...].astype(F32)
    hits, gate_rows = [], []
    for j in range(n):
        same = ids == EXP_DEV * peers[j]
        hits.append(jnp.sum(jnp.where(same, 1.0, 0.0), axis=0, keepdims=True))
        gate_rows.append(jnp.sum(jnp.where(same, gates, 0.0), axis=0, keepdims=True))
    pad = [jnp.zeros((128 - n, tok_count), F32)]
    hit_t = jnp.concatenate(hits + pad, axis=0)
    gate_t = jnp.concatenate(gate_rows + pad, axis=0)
    t_row = lax.broadcasted_iota(jnp.int32, (tok_count, tok_count), 0)
    t_col = lax.broadcasted_iota(jnp.int32, (tok_count, tok_count), 1)
    above = jnp.where(t_row < t_col, 1.0, 0.0).astype(BF16)
    eye = jnp.where(t_col == t_row, 1.0, 0.0).astype(BF16)
    rank_t = jnp.dot(hit_t.astype(BF16), above, preferred_element_type=F32)
    key_t = jnp.where(hit_t > 0.5, rank_t, -1.0)

    row_id = lax.broadcasted_iota(jnp.int32, (rows, tok_count), 0).astype(F32)
    for j in range(n):
        pick[j * rows:(j + 1) * rows, :] = jnp.where(row_id == key_t[j:j + 1, :], 1.0, 0.0)
    pick_all = pick[...].astype(BF16)

    def remote(src, dst, a_sem, b_sem, j):
        return pltpu.make_async_remote_copy(
            src_ref=src.at[j], dst_ref=dst.at[j], send_sem=a_sem.at[j], recv_sem=b_sem.at[j],
            device_id=(my_dp, peers[j]), device_id_type=MESH)

    def part(j, h):
        cut = (j, slice(None), pl.ds(h * half, half))
        return pltpu.make_async_remote_copy(
            src_ref=send.at[cut], dst_ref=recv.at[cut], send_sem=s_send.at[2 * j + h],
            recv_sem=s_recv.at[2 * j + h], device_id=(my_dp, peers[j]), device_id_type=MESH)

    out_copies = [[part(j, 0), part(j, 1)] if j else [] for j in range(n)]
    loads[0].wait()
    loads[1].wait()
    for h in range(2):
        for c in range(h * half, h * half + half, 512):
            sel_x = jnp.dot(pick_all, tok[:, c:c + 512], preferred_element_type=F32)
            sel_d = jnp.dot(pick_all, dy[:, c:c + 512], preferred_element_type=F32)
            for j in range(n):
                both = jnp.concatenate(
                    [sel_x[j * rows:(j + 1) * rows], sel_d[j * rows:(j + 1) * rows]], axis=0)
                if j == 0:
                    recv[0, :, c:c + 512] = both.astype(BF16)
                else:
                    send[j, :, c:c + 512] = both.astype(BF16)
        if h == 0:
            pl.semaphore_wait(barrier, n - 1 + dp - 1)
        for j in groups[1]:
            out_copies[j][h].start()

    key = lax.dot_general(
        eye, key_t.astype(BF16), (((1,), (1,)), ((), ())), preferred_element_type=F32)
    gsel = lax.dot_general(
        eye, gate_t.astype(BF16), (((1,), (1,)), ((), ())), preferred_element_type=F32)
    lanes = lax.broadcasted_iota(jnp.int32, (1, n * hi), 1).astype(F32)
    mat = jnp.zeros((tok_count, n * hi), F32)
    mat_r = jnp.zeros((tok_count, n * span), F32)
    lanes_r = lax.broadcasted_iota(jnp.int32, (1, n * span), 1).astype(F32)
    for j in range(n):
        there = key[:, j:j + 1] > -0.5
        spot = jnp.where(there, key[:, j:j + 1] + (hi * j), -1.0)
        mat = mat + jnp.where(lanes == spot, gsel[:, j:j + 1], 0.0)
        spot_r = jnp.where(there, key[:, j:j + 1] + (span * j + off), -1.0)
        mat_r = mat_r + jnp.where(lanes_r == spot_r, gsel[:, j:j + 1], 0.0)
    gl[...] = mat.astype(BF16)
    gr[...] = mat_r.astype(BF16)

    diag = (lax.broadcasted_iota(jnp.int32, (rows, 128), 0)
            == lax.broadcasted_iota(jnp.int32, (rows, 128), 1))
    loads[2].wait()
    loads[3].wait()
    total = jnp.zeros((1, width), F32)
    back_copies, gate_copies = [], []
    for number, group in enumerate(groups):
        for j in group:
            for copy in out_copies[j]:
                copy.wait_recv()
        g = len(group)
        xs = jnp.concatenate([recv[j, 0:hi, :] for j in group], axis=0)
        ds = jnp.concatenate([recv[j, lo:2 * rows, :] for j in group], axis=0)
        terms = [jnp.zeros((rows, 1), F32) for _ in group]
        for c in range(0, hidden, 256):
            act_all = jnp.dot(xs, wu[:, c:c + 256], preferred_element_type=F32)
            u_all = nt_dot(ds, wd[c:c + 256, :])
            grads = []
            for i in range(g):
                act = act_all[i * hi:i * hi + rows]
                u = u_all[i * span + off:i * span + off + rows]
                sig = jax.nn.sigmoid(act)
                hid = (act * sig).astype(BF16).astype(F32)
                terms[i] = terms[i] + jnp.sum(hid * u, axis=1, keepdims=True)
                grads.append(u * sig * (1.0 + act * (1.0 - sig)))
            agr[0:g * rows, c:c + 256] = jnp.concatenate(grads, axis=0).astype(BF16)
        for i, j in enumerate(group):
            line = jnp.sum(jnp.where(diag, terms[i], 0.0), axis=0, keepdims=True)
            line = jnp.broadcast_to(line, (8, 128))
            if j == 0:
                grecv[0] = line
            else:
                gsend[j] = line
                copy = remote(gsend, grecv, g_send, g_recv, j)
                copy.start()
                gate_copies.append(copy)
        grad_in = agr[0:g * rows, :]
        left = nt_dot(grad_in, wu[0:half, :])
        right = nt_dot(grad_in, wu[half:width, :])
        for i, j in enumerate(group):
            block = jnp.concatenate(
                [left[i * rows:(i + 1) * rows], right[i * rows:(i + 1) * rows]], axis=0)
            if j == 0:
                rsend[0] = block.astype(BF16)
                own = pltpu.make_async_copy(rsend.at[0], rrecv.at[0], local_sem.at[4])
                own.start()
            else:
                rsend[j] = block.astype(BF16)
                copy = remote(rsend, rrecv, r_send, r_recv, j)
                copy.start()
                back_copies.append(copy)
        for i, j in enumerate(group):
            total = total + jnp.sum(
                recv[j, 0:hi, :].astype(F32)[0:rows] * terms[i], axis=0, keepdims=True)
        if number == 0:
            for h in range(2):
                for j in groups[1]:
                    out_copies[j][h].wait_send()
                for j in groups[2]:
                    out_copies[j][h].start()

    cols[my_dp] = total
    col_copies = []
    for k in range(1, dp):
        copy = pltpu.make_async_remote_copy(
            src_ref=cols.at[my_dp], dst_ref=cols.at[my_dp], send_sem=c_send.at[k],
            recv_sem=c_recv.at[k], device_id=(lax.rem(my_dp + k, dp), me), device_id_type=MESH)
        copy.start()
        col_copies.append(copy)

    for copy in gate_copies:
        copy.wait_recv()
    gate_out = jnp.zeros(ids.shape, F32)
    for j in range(n):
        col = jnp.sum(jnp.where(diag, grecv[j, 0:1, :], 0.0), axis=1, keepdims=True)
        term = jnp.sum(pick[j * rows:(j + 1) * rows, :] * col, axis=0, keepdims=True)
        gate_out = gate_out + jnp.where(ids == EXP_DEV * peers[j], term, 0.0)
    gg_ref[...] = gate_out

    for k in range(1, dp):
        src = lax.rem(my_dp + dp - k, dp)
        pltpu.make_async_remote_copy(
            src_ref=cols.at[src], dst_ref=cols.at[src], send_sem=c_send.at[k],
            recv_sem=c_recv.at[k], device_id=(src, me), device_id_type=MESH).wait_recv()
    col = cols[0]
    for i in range(1, dp):
        col = col + cols[i]
    rg_ref[...] = col / F32(tok_count * dp)

    for j in groups[2]:
        for copy in out_copies[j]:
            copy.wait_send()
    own.wait()
    for copy in gate_copies + back_copies + col_copies:
        copy.wait_send()
    for copy in back_copies:
        copy.wait_recv()


def combine(n, rows, back, gl, gr, gg_in, rg_in, tg_ref, gg_ref, rg_ref):
    half = back.shape[2]
    hi = -(-rows // 16) * 16
    lo = rows // 16 * 16
    back_l = jnp.concatenate([back[j, 0:hi, :] for j in range(n)], axis=0)
    tg_ref[:, 0:half] = jnp.dot(gl[...], back_l, preferred_element_type=F32).astype(BF16)
    back_r = jnp.concatenate([back[j, lo:2 * rows, :] for j in range(n)], axis=0)
    tg_ref[:, half:2 * half] = jnp.dot(gr[...], back_r, preferred_element_type=F32).astype(BF16)
    gg_ref[...] = gg_in[...].astype(BF16)
    rg_ref[...] = rg_in[...]


def body(tokens, upstream, expert_ids, gate_weights, w_up, w_down):
    n = lax.axis_size("expert")
    dp = lax.axis_size("dp")
    tok_count, width = tokens.shape
    top = expert_ids.shape[1]
    hidden = w_up.shape[2]
    experts = EXP_DEV * n
    most = tok_count * top // experts + tok_count * top // (4 * experts)
    rows = -(-most // 8) * 8
    hi = -(-rows // 16) * 16
    span = 2 * rows - rows // 16 * 16
    groups = [(0,), tuple(range(1, n // 2 + 1)), tuple(range(n // 2 + 1, n))]
    biggest = max(len(g) for g in groups)
    hbm = pl.BlockSpec(memory_space=pltpu.HBM)
    vmem = pl.BlockSpec(memory_space=pltpu.VMEM)
    dma = pltpu.SemaphoreType.DMA
    back, gl, gr, gg, rg = pl.pallas_call(
        functools.partial(kernel, n, dp, rows, groups),
        out_shape=(
            jax.ShapeDtypeStruct((n, 2 * rows, width // 2), BF16),
            jax.ShapeDtypeStruct((tok_count, n * hi), BF16),
            jax.ShapeDtypeStruct((tok_count, n * span), BF16),
            jax.ShapeDtypeStruct((top, tok_count), F32),
            jax.ShapeDtypeStruct((1, width), F32),
        ),
        in_specs=[hbm, hbm, vmem, vmem, hbm, hbm],
        out_specs=(hbm,) + (vmem,) * 4,
        scratch_shapes=[
            pltpu.VMEM((tok_count, width), BF16),
            pltpu.VMEM((tok_count, width), BF16),
            pltpu.VMEM((width, hidden), BF16),
            pltpu.VMEM((hidden, width), BF16),
            pltpu.VMEM((n, 2 * rows, width), BF16),
            pltpu.VMEM((n, 2 * rows, width), BF16),
            pltpu.VMEM((n, 2 * rows, width // 2), BF16),
            pltpu.VMEM((n, 8, 128), F32),
            pltpu.VMEM((n, 8, 128), F32),
            pltpu.VMEM((-(-biggest * rows // 16) * 16, hidden), BF16),
            pltpu.VMEM((dp, 1, width), F32),
            pltpu.VMEM((n * rows, tok_count), F32),
            dma((5,)),
            dma((2 * n,)), dma((2 * n,)), dma((n,)), dma((n,)), dma((n,)), dma((n,)),
            dma((dp,)), dma((dp,)),
        ],
        compiler_params=pltpu.CompilerParams(
            collective_id=0, has_side_effects=True, vmem_limit_bytes=60 * 1024 * 1024),
        cost_estimate=pl.CostEstimate(
            flops=6 * n * rows * width * hidden, bytes_accessed=4 * width * hidden,
            transcendentals=n * rows * hidden),
    )(tokens, upstream, expert_ids.T, gate_weights.T, w_up[0], w_down[0])
    token_grads, gate_t, router = pl.pallas_call(
        functools.partial(combine, n, rows),
        out_shape=(
            jax.ShapeDtypeStruct((tok_count, width), BF16),
            jax.ShapeDtypeStruct((top, tok_count), BF16),
            jax.ShapeDtypeStruct((1, width), F32),
        ),
        in_specs=[vmem] * 5,
        out_specs=(vmem,) * 3,
        compiler_params=pltpu.CompilerParams(vmem_limit_bytes=60 * 1024 * 1024),
    )(back, gl, gr, gg, rg)
    return token_grads, gate_t.T, router


def solution(mesh):
    return jax.shard_map(
        body,
        mesh=mesh,
        in_specs=(
            P(("dp", "expert"), None),
            P(("dp", "expert"), None),
            P(("dp", "expert"), None),
            P(("dp", "expert"), None),
            P("expert", None, None),
            P("expert", None, None),
        ),
        out_specs=(P(("dp", "expert"), None), P(("dp", "expert"), None), P("expert", None)),
        check_vma=False,
    )
```

time: 39.7 us -> 35.1 us (0.88)
  local copies, waits for them, and re-layouts: 7.6 us -> 0 us
  Pallas kernels: 31.1 us -> 34.2 us
    unnamed x10 -> x0, local copies, waits for them, and re-layouts: 6.95 us -> none
    pallas_call x0 -> x1, Pallas kernels: none -> 2.23 us  [body(): pl.pallas_call(functools.partial(combine, n, rows), out_shape=(jax.ShapeD...]
    pallas_call x1, Pallas kernels: 31.1 us -> 32 us  [body(): pl.pallas_call(functools.partial(kernel, n, dp, rows, groups), out_shape=...]
    pallas_call x1 -> x0, local copies, waits for them, and re-layouts: 0.65 us -> none  [body(): pl.pallas_call(functools.partial(kernel, n, dp, rows, groups), out_shape=...]
where the time goes in v2:
time: 35.1 us; the launch traced here: 34.9 us
  Pallas kernels  34.2 us (97%)
  between operations  0.64 us (2%)
    pallas_call x1, Pallas kernels, body(): pl.pallas_call(functools.partial(kernel, n, dp, rows, groups), out_shape=...  32 us
    pallas_call x1, Pallas kernels, body(): pl.pallas_call(functools.partial(combine, n, rows), out_shape=(jax.ShapeD...  2.23 us

profile of v2, /device:TPU:0, one launch (start us, length us, event | category | flops | bytes accessed | tf_op | source)
XLA Modules:
  0.0 34.9 jit_solution(4188377827582990326)
XLA Ops:
  0.6 32.0 %shard_map.85 = (bf16[4,80,1024]{2,1,0:T(8,128)(2,1)}, bf16[128,192]{1,0:T(8,128)(2,1)}, bf16[128,192]{1,0:T(8,128)(2,1)}, f32[8,128]{1,0:T(8,128)}, f32[1,2048]{1,0:T(1,128)}) custom-call(bf16[128,2048]{1,0:T(8,128)(2,1)} %tok_hbm.1, bf16[128,2048]{1,0:T(8,128)(2,1)} %dy_hbm.1, s32[8,128]{1,0:T(8,128)} %bitcast.7, bf16[8,128]{1,0:T(8,128)(2,1)} %bitcast.8, ...), custom_call_target="tpu_custom_call" | custom-call | flops 1509949440 | bytes 6291456 | tf_op jit(solution)/shard_map/pallas_call | solution.py:254
  32.6 2.2 %shard_map.86 = (bf16[128,2048]{1,0:T(8,128)(2,1)}, bf16[8,128]{1,0:T(8,128)(2,1)}, f32[1,2048]{1,0:T(1,128)}) custom-call(bf16[4,80,1024]{2,1,0:T(8,128)(2,1)} %get-tuple-element.11.back, bf16[128,192]{1,0:T(8,128)(2,1)} %get-tuple-element.12.gl, bf16[128,192]{1,0:T(8,128)(2,1)} %get-tuple-element.13.gr, f32[8,128]{1,0:T(8,128)} %get-tuple-element.14.gg_in, ...), custom_call_target="tpu_custom_call" | custom-call | tf_op jit(solution)/shard_map/pallas_call | solution.py:288

commit v3 on v2

--- a/solution.py
+++ b/solution.py
@@ -45,8 +45,8 @@
         for i, (src, dst) in enumerate(
             ((tok_hbm, tok), (dy_hbm, dy), (wu_hbm, wu), (wd_hbm, wd)))
     ]
-    for load in loads:
-        load.start()
+    loads[0].start()
+    loads[1].start()
 
     barrier = pltpu.get_barrier_semaphore()
     for j in range(1, n):
@@ -91,6 +91,8 @@
     out_copies = [[part(j, 0), part(j, 1)] if j else [] for j in range(n)]
     loads[0].wait()
     loads[1].wait()
+    loads[2].start()
+    loads[3].start()
     for h in range(2):
         for c in range(h * half, h * half + half, 512):
             sel_x = jnp.dot(pick_all, tok[:, c:c + 512], preferred_element_type=F32)
@@ -128,8 +130,13 @@
             == lax.broadcasted_iota(jnp.int32, (rows, 128), 1))
     loads[2].wait()
     loads[3].wait()
+    for h in range(2):
+        for j in groups[1]:
+            out_copies[j][h].wait_send()
+        for j in groups[2]:
+            out_copies[j][h].start()
     total = jnp.zeros((1, width), F32)
-    back_copies, gate_copies = [], []
+    back_copies, gate_copies, col_copies = [], [], []
     for number, group in enumerate(groups):
         for j in group:
             for copy in out_copies[j]:
@@ -160,39 +167,37 @@
                 copy = remote(gsend, grecv, g_send, g_recv, j)
                 copy.start()
                 gate_copies.append(copy)
-        grad_in = agr[0:g * rows, :]
-        left = nt_dot(grad_in, wu[0:half, :])
-        right = nt_dot(grad_in, wu[half:width, :])
-        for i, j in enumerate(group):
-            block = jnp.concatenate(
-                [left[i * rows:(i + 1) * rows], right[i * rows:(i + 1) * rows]], axis=0)
-            if j == 0:
-                rsend[0] = block.astype(BF16)
-                own = pltpu.make_async_copy(rsend.at[0], rrecv.at[0], local_sem.at[4])
-                own.start()
-            else:
-                rsend[j] = block.astype(BF16)
-                copy = remote(rsend, rrecv, r_send, r_recv, j)
-                copy.start()
-                back_copies.append(copy)
         for i, j in enumerate(group):
             total = total + jnp.sum(
                 recv[j, 0:hi, :].astype(F32)[0:rows] * terms[i], axis=0, keepdims=True)
+        if number == len(groups) - 1:
+            cols[my_dp] = total
+            for k in range(1, dp):
+                copy = pltpu.make_async_remote_copy(
+                    src_ref=cols.at[my_dp], dst_ref=cols.at[my_dp], send_sem=c_send.at[k],
+                    recv_sem=c_recv.at[k], device_id=(lax.rem(my_dp + k, dp), me), device_id_type=MESH)
+                copy.start()
+                col_copies.append(copy)
+        grad_in = agr[0:g * rows, :]
+        for q in range(2):
+            c = q * (half // 2)
+            left = nt_dot(grad_in, wu[c:c + half // 2, :])
+            right = nt_dot(grad_in, wu[half + c:half + c + half // 2, :])
+            for i, j in enumerate(group):
+                block = jnp.concatenate(
+                    [left[i * rows:(i + 1) * rows], right[i * rows:(i + 1) * rows]], axis=0)
+                rsend[j, :, c:c + half // 2] = block.astype(BF16)
+                if j:
+                    cut = (j, slice(None), pl.ds(c, half // 2))
+                    copy = pltpu.make_async_remote_copy(
+                        src_ref=rsend.at[cut], dst_ref=rrecv.at[cut],
+                        send_sem=r_send.at[2 * j + q], recv_sem=r_recv.at[2 * j + q],
+                        device_id=(my_dp, peers[j]), device_id_type=MESH)
+                    copy.start()
+                    back_copies.append(copy)
         if number == 0:
-            for h in range(2):
-                for j in groups[1]:
-                    out_copies[j][h].wait_send()
-                for j in groups[2]:
-                    out_copies[j][h].start()
-
-    cols[my_dp] = total
-    col_copies = []
-    for k in range(1, dp):
-        copy = pltpu.make_async_remote_copy(
-            src_ref=cols.at[my_dp], dst_ref=cols.at[my_dp], send_sem=c_send.at[k],
-            recv_sem=c_recv.at[k], device_id=(lax.rem(my_dp + k, dp), me), device_id_type=MESH)
-        copy.start()
-        col_copies.append(copy)
+            own = pltpu.make_async_copy(rsend.at[0], rrecv.at[0], local_sem.at[4])
+            own.start()
 
     for copy in gate_copies:
         copy.wait_recv()
@@ -276,7 +281,7 @@
             pltpu.VMEM((dp, 1, width), F32),
             pltpu.VMEM((n * rows, tok_count), F32),
             dma((5,)),
-            dma((2 * n,)), dma((2 * n,)), dma((n,)), dma((n,)), dma((n,)), dma((n,)),
+            dma((2 * n,)), dma((2 * n,)), dma((2 * n,)), dma((2 * n,)), dma((n,)), dma((n,)),
             dma((dp,)), dma((dp,)),
         ],
         compiler_params=pltpu.CompilerParams(

time: 35.1 us -> 34.9 us (level)
  no operation moved by 1% of the time
where the time goes in v3:
time: 34.9 us; the launch traced here: 34.7 us
  Pallas kernels  34.1 us (98%)
  between operations  0.64 us (2%)
    pallas_call x1, Pallas kernels, body(): pl.pallas_call(functools.partial(kernel, n, dp, rows, groups), out_shape=...  31.8 us
    pallas_call x1, Pallas kernels, body(): pl.pallas_call(functools.partial(combine, n, rows), out_shape=(jax.ShapeD...  2.24 us

profile of v3, /device:TPU:0, one launch (start us, length us, event | category | flops | bytes accessed | tf_op | source)
XLA Modules:
  0.0 34.7 jit_solution(7720745018922534463)
XLA Ops:
  0.6 31.8 %shard_map.85 = (bf16[4,80,1024]{2,1,0:T(8,128)(2,1)}, bf16[128,192]{1,0:T(8,128)(2,1)}, bf16[128,192]{1,0:T(8,128)(2,1)}, f32[8,128]{1,0:T(8,128)}, f32[1,2048]{1,0:T(1,128)}) custom-call(bf16[128,2048]{1,0:T(8,128)(2,1)} %tok_hbm.1, bf16[128,2048]{1,0:T(8,128)(2,1)} %dy_hbm.1, s32[8,128]{1,0:T(8,128)} %bitcast.7, bf16[8,128]{1,0:T(8,128)(2,1)} %bitcast.8, ...), custom_call_target="tpu_custom_call" | custom-call | flops 1509949440 | bytes 6291456 | tf_op jit(solution)/shard_map/pallas_call | solution.py:259
  32.5 2.2 %shard_map.86 = (bf16[128,2048]{1,0:T(8,128)(2,1)}, bf16[8,128]{1,0:T(8,128)(2,1)}, f32[1,2048]{1,0:T(1,128)}) custom-call(bf16[4,80,1024]{2,1,0:T(8,128)(2,1)} %get-tuple-element.11.back, bf16[128,192]{1,0:T(8,128)(2,1)} %get-tuple-element.12.gl, bf16[128,192]{1,0:T(8,128)(2,1)} %get-tuple-element.13.gr, f32[8,128]{1,0:T(8,128)} %get-tuple-element.14.gg_in, ...), custom_call_target="tpu_custom_call" | custom-call | tf_op jit(solution)/shard_map/pallas_call | solution.py:293
